TPU v7x, 32 devices: a whole 2x2x4 slice. The times are simulated.
32 devices in a mesh: grp: 2 (over y), ctx: 4 (over z), head: 4 (over x, core).
Axes of the slice: x: 2, y: 2, z: 4, core: 2. Of those that a mesh axis runs over, the one named last changes fastest.
Arguments:
- query_raw: bfloat16 [2048, 2048], P(('grp', 'ctx'), 'head'), parts along dimension 0, may hold values from -6 to 6
- key_raw: bfloat16 [2048, 2048], P(('grp', 'ctx'), 'head'), parts along dimension 0, may hold values from -6 to 6
- value_raw: bfloat16 [2048, 4096], P(('grp', 'ctx'), 'head'), parts along dimension 0, may hold values from -6 to 6
- out_gate: bfloat16 [2048, 4096], P(('grp', 'ctx'), 'head'), parts along dimension 0, may hold values from -6 to 6
- conv_query: float32 [4, 2048], P(None, 'head'), may hold values from -3 to 3
- conv_key: float32 [4, 2048], P(None, 'head'), may hold values from -3 to 3
- conv_value: float32 [4, 4096], P(None, 'head'), may hold values from -3 to 3
- decay_log: float32 [2048, 32], P(('grp', 'ctx'), 'head'), parts along dimension 0, may hold values from -1.6 to 0
- write_beta: float32 [2048, 32], P(('grp', 'ctx'), 'head'), parts along dimension 0, may hold values from 0.02 to 0.9
- norm_gain: float32 [128], replicated, may hold values from 0.5 to 1.5
- query_heads: bfloat16 [2048, 4096], P(('grp', 'ctx'), 'head'), parts along dimension 0, may hold values from -7 to 7
- gate_heads: bfloat16 [2048, 4096], P(('grp', 'ctx'), 'head'), parts along dimension 0, may hold values from -6 to 6
- key_heads: bfloat16 [2048, 512], P(('grp', 'ctx')), parts along dimension 0, may hold values from -7 to 7
- value_heads: bfloat16 [2048, 512], P(('grp', 'ctx')), parts along dimension 0, may hold values from -6 to 6
- query_gain: float32 [256], replicated, may hold values from 0.7 to 4.5
- key_gain: float32 [256], replicated, may hold values from 0.7 to 4.5
Outputs:
- deltanet_out: bfloat16 [2048, 4096], P(('grp', 'ctx'), 'head'), parts along dimension 0
- attention_out: bfloat16 [2048, 4096], P(('grp', 'ctx'), 'head'), parts along dimension 0
There are 2 independent parts, one for each index of `grp`. A program takes and returns all parts, laid end to end along the dimension named above; an argument that names none is the same for every part. Nothing has to cross between parts.
All inputs are finite; a program needn't handle non-finite values.
Results may differ from a plain program's by a relative error of at most 0.01.
The roundings to bfloat16 on the way count: a program that leaves them out, or rounds other values in their place, can miss the bound.
Values may be sent and summed in bfloat16 or wider, within the bound.
A program may use at most 128 MiB of HBM per device.

v0:
```python
import jax
import jax.numpy as jnp
from jax import lax
from jax.sharding import PartitionSpec as P

D_K = 128
D_V = 128
K_HEADS = 16
VALUE_HEAD_COUNT = 32
CONV = 4
SPAN = 64
Q_HEADS = 16
KV_HEADS = 2
HEAD_DIM = 256


HIGHEST = lax.Precision.HIGHEST
ROPE_THETA = 10000000.0


def from_behind(value, axis, steps):
    count = lax.axis_size(axis)
    initial, last = (max(0, -steps), min(count, count - steps))
    return lax.ppermute(value, axis, [(source, source + steps) for source in range(initial, last)])


def matmul_heads(left, right):
    return jnp.einsum("hij,hjk->hik", left, right, precision=HIGHEST)


def unit_lower_inverse(strict_part):
    length = strict_part.shape[-1]
    identity = jnp.eye(length, dtype=jnp.float32)
    power_term = -strict_part
    inverse = identity + power_term
    for level in range(1, max(1, (length - 1).bit_length())):
        power_term = matmul_heads(power_term, power_term)
        inverse = matmul_heads(inverse, identity + power_term)
    return inverse


def delta_span(memory, queries, keys_in, values_in, decay_part, beta_part, with_output):
    length = keys_in.shape[1]
    cumulative = jnp.cumsum(decay_part, axis=1)
    lower_incl = jnp.tril(jnp.ones((length, length), dtype=bool))
    strict_mask = jnp.tril(jnp.ones((length, length), dtype=jnp.float32), -1)
    spacing = jnp.where(lower_incl, cumulative[:, :, None] - cumulative[:, None, :], 0.0)
    within = jnp.where(lower_incl, jnp.exp(spacing), 0.0)
    key_gram = matmul_heads(keys_in, jnp.swapaxes(keys_in, 1, 2))
    coupling = beta_part[:, :, None] * key_gram * within * strict_mask
    inverse = unit_lower_inverse(coupling)
    decay_now = jnp.exp(cumulative)
    weights_left = matmul_heads(inverse, (beta_part * decay_now)[:, :, None] * keys_in)
    targets = matmul_heads(inverse, beta_part[:, :, None] * values_in)
    fresh = targets - matmul_heads(weights_left, memory)
    last_sum = cumulative[:, -1]
    scaled_keys = keys_in * jnp.exp(last_sum[:, None] - cumulative)[:, :, None]
    carried = jnp.exp(last_sum)[:, None, None] * memory + matmul_heads(
        jnp.swapaxes(scaled_keys, 1, 2), fresh
    )
    if with_output:
        inner = matmul_heads(queries, jnp.swapaxes(keys_in, 1, 2)) * within
        output = matmul_heads(queries * decay_now[:, :, None], memory) + matmul_heads(inner, fresh)
        return (carried, output)
    return (carried, None)


def run_spans(memory, queries, keys_in, values_in, decay_log, write_beta, with_output):
    row_count = keys_in.shape[0]
    span_count = row_count // SPAN

    def shaped(array):
        return array.reshape((span_count, SPAN) + array.shape[1:])

    def advance(memory_in, pieces):
        span_query, span_key, span_value, span_decay, span_beta = pieces
        return delta_span(
            memory_in,
            jnp.swapaxes(span_query, 0, 1),
            jnp.swapaxes(span_key, 0, 1),
            jnp.swapaxes(span_value, 0, 1),
            span_decay.T,
            span_beta.T,
            with_output,
        )

    final, outputs = lax.scan(
        advance,
        memory,
        (
            shaped(queries),
            shaped(keys_in),
            shaped(values_in),
            shaped(decay_log),
            shaped(write_beta),
        ),
    )
    if with_output:
        outputs = jnp.swapaxes(outputs, 1, 2).reshape(row_count, outputs.shape[1], outputs.shape[3])
    return (final, outputs)


def conv_silu(rim_block, local_block, kernel):
    taps = kernel.shape[0]
    length = local_block.shape[0]
    padded = jnp.concatenate([rim_block, local_block], 0).astype(jnp.float32)
    summed = kernel[0] * padded[0:length]
    for tap_index in range(1, taps):
        summed = summed + kernel[tap_index] * padded[tap_index : tap_index + length]
    return jax.nn.silu(summed)


def unit_rows(matrix):
    return matrix * lax.rsqrt(jnp.sum(matrix * matrix, -1, keepdims=True) + 1e-06)


def delta_inputs(query_conv, key_conv, value_conv):
    row_count = query_conv.shape[0]
    repeats = VALUE_HEAD_COUNT // K_HEADS
    queries = unit_rows(query_conv.reshape(row_count, -1, D_K)) * D_K ** (-0.5)
    keys_in = unit_rows(key_conv.reshape(row_count, -1, D_K))
    queries = jnp.repeat(queries, repeats, axis=1)
    keys_in = jnp.repeat(keys_in, repeats, axis=1)
    values_in = value_conv.reshape(row_count, -1, D_V)
    return (queries, keys_in, values_in)


def gated_norm(output, gate_raw, gain):
    normed = output * lax.rsqrt(jnp.mean(output * output, -1, keepdims=True) + 1e-06) * gain
    gated = normed.reshape(gate_raw.shape) * jax.nn.silu(gate_raw.astype(jnp.float32))
    return gated.astype(jnp.bfloat16)


def rope_norm(heads_in, gain, positions):
    normed = heads_in * lax.rsqrt(jnp.mean(heads_in * heads_in, -1, keepdims=True) + 1e-06) * gain
    half_width = heads_in.shape[-1] // 8
    frequency = ROPE_THETA ** (-jnp.arange(half_width, dtype=jnp.float32) / half_width)
    angles = positions.astype(jnp.float32)[:, None] * frequency[None, :]
    cosine = jnp.cos(angles)[:, None, :]
    sine = jnp.sin(angles)[:, None, :]
    first_part = normed[..., :half_width]
    second_part = normed[..., half_width : 2 * half_width]
    rotated = jnp.concatenate(
        [
            first_part * cosine - second_part * sine,
            second_part * cosine + first_part * sine,
            normed[..., 2 * half_width :],
        ],
        -1,
    )
    return rotated.astype(jnp.bfloat16)


def body(
    query_raw,
    key_raw,
    value_raw,
    out_gate,
    conv_query,
    conv_key,
    conv_value,
    decay_log,
    write_beta,
    norm_gain,
    query_heads,
    gate_heads,
    key_heads,
    value_heads,
    query_gain,
    key_gain,
):
    row_count = query_raw.shape[0]
    ctx_index = lax.axis_index("ctx")
    rim_count = CONV - 1
    rim_rows = from_behind(
        jnp.concatenate(
            [
                query_raw[row_count - rim_count :],
                key_raw[row_count - rim_count :],
                value_raw[row_count - rim_count :],
            ],
            1,
        ),
        "ctx",
        1,
    )
    split_first = query_raw.shape[1]
    split_second = split_first + key_raw.shape[1]
    query_conv = conv_silu(rim_rows[:, :split_first], query_raw, conv_query)
    key_conv = conv_silu(rim_rows[:, split_first:split_second], key_raw, conv_key)
    value_conv = conv_silu(rim_rows[:, split_second:], value_raw, conv_value)
    queries, keys_in, values_in = delta_inputs(query_conv, key_conv, value_conv)
    value_count = values_in.shape[1]
    identity = jnp.broadcast_to(jnp.eye(D_K, dtype=jnp.float32), (value_count, D_K, D_K))
    extended = jnp.concatenate(
        [values_in, jnp.zeros((row_count, value_count, D_K), jnp.float32)], -1
    )
    start_memory = jnp.concatenate([jnp.zeros((value_count, D_K, D_V), jnp.float32), identity], -1)
    summary, unused = run_spans(
        start_memory, queries, keys_in, extended, decay_log, write_beta, False
    )
    offset = summary[..., :D_V]
    transfer = summary[..., D_V:]

    def relay(turn_index, carried):
        return from_behind(
            (matmul_heads(transfer, carried) + offset).astype(jnp.bfloat16), "ctx", 1
        ).astype(jnp.float32)

    incoming = lax.fori_loop(0, lax.axis_size("ctx") - 1, relay, jnp.zeros_like(offset))
    unused_final, delta_out = run_spans(
        incoming, queries, keys_in, values_in, decay_log, write_beta, True
    )
    deltanet_out = gated_norm(delta_out, out_gate, norm_gain)
    head_count = query_heads.shape[1] // HEAD_DIM
    group_size = Q_HEADS // KV_HEADS
    head_index = lax.axis_index("head")
    kv_index = head_index * head_count // group_size
    positions = ctx_index * row_count + jnp.arange(row_count, dtype=jnp.int32)
    query_rot = rope_norm(
        query_heads.astype(jnp.float32).reshape(row_count, head_count, HEAD_DIM),
        query_gain,
        positions,
    )
    chosen_keys = lax.dynamic_index_in_dim(
        key_heads.reshape(row_count, KV_HEADS, HEAD_DIM), kv_index, 1, True
    )
    key_rot = rope_norm(chosen_keys.astype(jnp.float32), key_gain, positions)[:, 0]
    chosen_values = lax.dynamic_index_in_dim(
        value_heads.reshape(row_count, KV_HEADS, HEAD_DIM), kv_index, 1, False
    )
    stacked = jnp.stack([key_rot, chosen_values])
    score_scale = HEAD_DIM ** (-0.5)

    def attend_block(running, block_keys, block_values, key_start):
        running_max, totals, mixed_sum = running
        scores = (
            jnp.einsum("rhd,pd->hrp", query_rot, block_keys, preferred_element_type=jnp.float32)
            * score_scale
        )
        key_pos = key_start + jnp.arange(block_keys.shape[0], dtype=jnp.int32)
        allowed = (key_pos[None, :] <= positions[:, None]) & (key_pos[None, :] >= 0)
        masked = jnp.where(allowed[None], scores, -1e30)
        new_max = jnp.maximum(running_max, jnp.max(masked, -1))
        expos = jnp.where(allowed[None], jnp.exp(masked - new_max[..., None]), 0.0)
        factor = jnp.exp(running_max - new_max)
        totals = totals * factor + jnp.sum(expos, -1)
        mixed_sum = mixed_sum * factor[..., None] + jnp.einsum(
            "hrp,pd->hrd",
            expos.astype(jnp.bfloat16),
            block_values,
            preferred_element_type=jnp.float32,
        )
        return (new_max, totals, mixed_sum)

    initial = (
        jnp.full((head_count, row_count), -1e30, jnp.float32),
        jnp.zeros((head_count, row_count), jnp.float32),
        jnp.zeros((head_count, row_count, HEAD_DIM), jnp.float32),
    )
    running = initial
    shard_piece = lax.all_gather(stacked, "ctx", axis=1, tiled=True)
    block_count = shard_piece.shape[1] // row_count

    def one_block(running_in, block_index):
        first_row = block_index * row_count
        key_block = lax.dynamic_slice_in_dim(shard_piece, first_row, row_count, 1)
        return (attend_block(running_in, key_block[0], key_block[1], first_row), None)

    running, unused_blocks = lax.scan(one_block, running, jnp.arange(block_count, dtype=jnp.int32))
    running_max, totals, mixed_sum = running
    heads_out = mixed_sum / totals[..., None]
    gated = jnp.swapaxes(heads_out, 0, 1).reshape(
        row_count, head_count * HEAD_DIM
    ) * jax.nn.sigmoid(gate_heads.astype(jnp.float32))
    return (deltanet_out, gated.astype(jnp.bfloat16))


def solution(mesh):
    placed = (
        P(("grp", "ctx"), "head"),
        P(("grp", "ctx"), "head"),
        P(("grp", "ctx"), "head"),
        P(("grp", "ctx"), "head"),
        P(None, "head"),
        P(None, "head"),
        P(None, "head"),
        P(("grp", "ctx"), "head"),
        P(("grp", "ctx"), "head"),
        P(),
        P(("grp", "ctx"), "head"),
        P(("grp", "ctx"), "head"),
        P(("grp", "ctx"), None),
        P(("grp", "ctx"), None),
        P(),
        P(),
    )
    return jax.shard_map(
        body,
        mesh=mesh,
        in_specs=placed,
        out_specs=(P(("grp", "ctx"), "head"), P(("grp", "ctx"), "head")),
        check_vma=False,
    )
```

profile of v0, /device:TPU:24, one launch (start us, length us, event | category | flops | bytes accessed | tf_op | source)
XLA Modules:
  0.0 175.2 jit_solution(862951669595631486)
XLA Ops:
  11.3 1.3 collective-permute-start.1
  15.0 1.9 %collective-permute-done.1 = bf16[3,2048]{1,0:T(4,128)(2,1)S(1)} collective-permute-done((bf16[3,2048]{1,0:T(4,128)(2,1)S(1)}, bf16[3,2048]{1,0:T(4,128)(2,1)S(1)}, u32[]{:S(2)}, u32[]{:S(2)}) %collective-permute-start.1) | collective-permute-done | bytes 12320 | tf_op jit(solution)/shard_map/ppermute | solution.py:24
  21.3 1.6 concatenate.45
  23.0 38.9 %while.48 = (s32[]{:T(128)}, f32[8,128,256]{2,1,0:T(8,128)S(1)}, f32[4,64,8]{1,2,0:T(8,128)S(1)}, f32[4,64,8,128]{3,1,2,0:T(8,128)S(1)}, f32[4,64,8]{1,2,0:T(8,1...) while((s32[]{:T(128)}, f32[8,128,256]{2,1,0:T(8,128)S(1)}, f32[4,64,8]{1,2,0:T(8,128)S(1)}, ...), condition=%wide.region_3.4_spmd, body=%wide.region_1.3_spmd.sunk | while | flops 857035328 | bytes 12392717 | solution.py:87
  31.2 1.5 convolution_add_fusion.13
  40.9 1.5 convolution_add_fusion.13
  50.6 1.5 convolution_add_fusion.13
  60.3 1.5 convolution_add_fusion.13
  64.3 1.5 multiply_multiply_fusion
  66.6 30.6 %while.50 = (s32[]{:T(128)}, f32[8,128,128]{2,1,0:T(8,128)S(1)}, f32[8,128,128]{2,1,0:T(8,128)S(1)}, f32[8,128,128]{2,1,0:T(8,128)S(1)}, s32[]{:T(128)}, /*index=5*/s32[]{:T(128)}) while((s32[]{:T(128)}, f32[8,128,128]{2,1,0:T(8,128)S(1)}, f32[8,128,128]{2,1,0:T(8,128)S(1)}, f32[8,128,128]{2,1,0:T(8,128)S(1)}, s32[]{:T(128)}, ...), condition=%wide.region_5.6_spmd.clone, body=%wide.region_4.5_spmd.clone.sunk | while | flops 201850880 | bytes 3670135 | solution.py:210
  66.6 1.4 fusion.380
  69.2 7.7 %collective-permute-done = bf16[8,128,128]{2,1,0:T(8,128)(2,1)S(1)} collective-permute-done((bf16[8,128,128]{2,1,0:T(8,128)(2,1)}, bf16[8,128,128]{2,1,0:T(8,128)(2,1)S(1)}, u32[]{:S(2)}, u32[]{:S(2)}) %collective-permute-start) | collective-permute-done | bytes 262176 | tf_op jit(solution)/shard_map/while/body/eval_jaxpr/ppermute | solution.py:24
  77.0 1.4 fusion.380
  79.7 7.5 %collective-permute-done = bf16[8,128,128]{2,1,0:T(8,128)(2,1)S(1)} collective-permute-done((bf16[8,128,128]{2,1,0:T(8,128)(2,1)}, bf16[8,128,128]{2,1,0:T(8,128)(2,1)S(1)}, u32[]{:S(2)}, u32[]{:S(2)}) %collective-permute-start) | collective-permute-done | bytes 262176 | tf_op jit(solution)/shard_map/while/body/eval_jaxpr/ppermute | solution.py:24
  87.3 1.4 fusion.380
  89.9 7.2 %collective-permute-done = bf16[8,128,128]{2,1,0:T(8,128)(2,1)S(1)} collective-permute-done((bf16[8,128,128]{2,1,0:T(8,128)(2,1)}, bf16[8,128,128]{2,1,0:T(8,128)(2,1)S(1)}, u32[]{:S(2)}, u32[]{:S(2)}) %collective-permute-start) | collective-permute-done | bytes 262176 | tf_op jit(solution)/shard_map/while/body/eval_jaxpr/ppermute | solution.py:24
  98.3 45.1 %while.49 = (s32[]{:T(128)}, f32[8,128,128]{2,1,0:T(8,128)S(1)}, f32[4,8,64,128]{3,2,1,0:T(8,128)}, f32[4,64,8]{1,2,0:T(8,128)S(1)}, f32[4,64,8,128]{3,1,2,0:T(8...) while((s32[]{:T(128)}, f32[8,128,128]{2,1,0:T(8,128)S(1)}, ...), condition=%wide.region_9.10_spmd, body=%wide.region_7.9_spmd.sunk | while | flops 806572608 | bytes 11630369 | solution.py:87
  143.4 1.7 multiply_reduce_fusion
  146.8 1.4 fusion.106
  148.3 17.8 %while.51 = (s32[]{:T(128)}, f32[4,256]{1,0:T(4,128)S(1)}, f32[4,256]{1,0:T(4,128)S(1)}, f32[4,256,256]{2,1,0:T(8,128)S(1)}, s32[4]{0:T(128)S(1)}, /*index=5*/bf...) while((s32[]{:T(128)}, f32[4,256]{1,0:T(4,128)S(1)}, ...), condition=%wide.region_16.17_spmd.clone, body=%wide.region_13.16_spmd.clone.sunk | while | flops 271718400 | bytes 6361831 | solution.py:270
  151.2 1.5 convolution_add_fusion.16
  155.7 1.5 convolution_add_fusion.16
  160.1 1.5 convolution_add_fusion.16
  164.6 1.5 convolution_add_fusion.16
  (364 shorter events, 108.2 us)
Async XLA Ops:
  7.2 6.8 %copy-start = (f32[128]{0:T(128)S(1)}, f32[128]{0:T(128)}, u32[]{:S(2)}) copy-start(f32[128]{0:T(128)} %param.33) | copy-start | bytes 1540
  7.2 2.2 %copy-start.14 = (bf16[256,512]{1,0:T(8,128)(2,1)S(1)}, bf16[256,512]{1,0:T(8,128)(2,1)}, u32[]{:S(2)}) copy-start(bf16[256,512]{1,0:T(8,128)(2,1)} %param.37) | copy-start | bytes 786436
  7.2 141.1 %all-gather.2.cloned.1.call-start = ((), (), s32[]{:S(2)}) async-start(), calls=%async_computation | async-start | bytes 1310720 | tf_op jit(solution)/shard_map/all_gather | solution.py:262
  8.4 2.8 %copy-start.13 = (bf16[256,512]{1,0:T(8,128)(2,1)S(1)}, bf16[256,512]{1,0:T(8,128)(2,1)}, u32[]{:S(2)}) copy-start(bf16[256,512]{1,0:T(8,128)(2,1)} %param.24) | copy-start | bytes 786436
  8.5 2.8 %copy-start.12 = (bf16[256,512]{1,0:T(8,128)(2,1)S(1)}, bf16[256,512]{1,0:T(8,128)(2,1)}, u32[]{:S(2)}) copy-start(bf16[256,512]{1,0:T(8,128)(2,1)} %param.25) | copy-start | bytes 786436
  9.3 3.5 %copy-start.9 = (bf16[256,1024]{1,0:T(8,128)(2,1)S(1)}, bf16[256,1024]{1,0:T(8,128)(2,1)}, u32[]{:S(2)}) copy-start(bf16[256,1024]{1,0:T(8,128)(2,1)} %param.34) | copy-start | bytes 1572868
  10.5 2.7 %copy-start.20 = (f32[256]{0:T(256)S(1)}, f32[256]{0:T(256)}, u32[]{:S(2)}) copy-start(f32[256]{0:T(256)} %param.38) | copy-start | bytes 3076
  11.3 5.6 %collective-permute-start.1 = (bf16[3,2048]{1,0:T(4,128)(2,1)S(1)}, bf16[3,2048]{1,0:T(4,128)(2,1)S(1)}, u32[]{:S(2)}, u32[]{:S(2)}) collective-permute-start(bf16[3,2048]{1,0:T(4,128)(2,1)S(1)} %pad_maximum_fusion.2), channel_id=1, source_target_pairs={{0,4},{4,8},{8,12},{1,5},{5,9},{9,13},{2,6},{6,10},{10,14},{3,7},{... | collective-permute-start | bytes 36872 | tf_op jit(solution)/shard_map/ppermute | solution.py:24
  13.2 0.7 copy-start.15
  13.2 0.7 copy-start.19
  14.0 0.8 copy-start.17
  19.3 1.0 copy-start.8
  21.3 1.6 copy-start.5
  61.9 1.1 copy-start.4
  63.5 0.8 copy-start.6
  64.3 2.3 %copy-start.2 = (f32[8,128,128]{2,1,0:T(8,128)S(1)}, f32[8,128,128]{2,1,0:T(8,128)}, u32[]{:S(2)}) copy-start(f32[8,128,128]{2,1,0:T(8,128)} %get-tuple-element.611) | copy-start | bytes 1572868
  64.3 2.3 %copy-start.3 = (f32[8,128,128]{2,1,0:T(8,128)S(1)}, f32[8,128,128]{2,1,0:T(8,128)}, u32[]{:S(2)}) copy-start(f32[8,128,128]{2,1,0:T(8,128)} %get-tuple-element.610) | copy-start | bytes 1572868
  68.0 9.0 %collective-permute-start = (bf16[8,128,128]{2,1,0:T(8,128)(2,1)}, bf16[8,128,128]{2,1,0:T(8,128)(2,1)S(1)}, u32[]{:S(2)}, u32[]{:S(2)}) collective-permute-start(bf16[8,128,128]{2,1,0:T(8,128)(2,1)} %fusion.380), channel_id=1, source_target_pairs={{0,4},{4,8},{8,12},{1,5},{5,9},{9,13},{2,6},{6,10},{10,14},{3,7},{... | collective-permute-start | bytes 786440 | tf_op jit(solution)/shard_map/while/body/eval_jaxpr/ppermute | solution.py:24
  78.4 8.8 %collective-permute-start = (bf16[8,128,128]{2,1,0:T(8,128)(2,1)}, bf16[8,128,128]{2,1,0:T(8,128)(2,1)S(1)}, u32[]{:S(2)}, u32[]{:S(2)}) collective-permute-start(bf16[8,128,128]{2,1,0:T(8,128)(2,1)} %fusion.380), channel_id=1, source_target_pairs={{0,4},{4,8},{8,12},{1,5},{5,9},{9,13},{2,6},{6,10},{10,14},{3,7},{... | collective-permute-start | bytes 786440 | tf_op jit(solution)/shard_map/while/body/eval_jaxpr/ppermute | solution.py:24
  88.7 8.5 %collective-permute-start = (bf16[8,128,128]{2,1,0:T(8,128)(2,1)}, bf16[8,128,128]{2,1,0:T(8,128)(2,1)S(1)}, u32[]{:S(2)}, u32[]{:S(2)}) collective-permute-start(bf16[8,128,128]{2,1,0:T(8,128)(2,1)} %fusion.380), channel_id=1, source_target_pairs={{0,4},{4,8},{8,12},{1,5},{5,9},{9,13},{2,6},{6,10},{10,14},{3,7},{... | collective-permute-start | bytes 786440 | tf_op jit(solution)/shard_map/while/body/eval_jaxpr/ppermute | solution.py:24
  143.4 1.8 %copy-start.7 = (f32[4,8,64,128]{3,2,1,0:T(8,128)S(1)}, f32[4,8,64,128]{3,2,1,0:T(8,128)}, u32[]{:S(2)}) copy-start(f32[4,8,64,128]{3,2,1,0:T(8,128)} %get-tuple-element.143) | copy-start | bytes 3145732
  145.8 1.0 copy-start.10
  146.8 1.4 copy-start.1
  166.3 1.0 copy-start.11
  (2 other events, 1.4 us)
Sparse Core Ops, SparseCore 0:
  10.6 28.1 all-gather.1
where the time goes:
time: 178 us; the launch traced here: 175 us
  matrix products  84.6 us (48%)
  local copies, waits for them, and re-layouts  25.4 us (14%)
  waiting for transfers between devices  24.4 us (14%)
  other arithmetic  16.5 us (9%)
  between operations  14.7 us (8%)
  starting transfers between devices  5.17 us (3%)
  loops' own time  4.5 us (3%)
    dot_general x135, matrix products, matmul_heads(): return jnp.einsum('hij,hjk->hik', left, right, precision=HIGHEST)  73.6 us
    ppermute x4, waiting for transfers between devices, from_behind(): lax.ppermute(value, axis, [(source, source + steps) for source in range(i...  24.4 us
    dynamic_slice x8, local copies, waits for them, and re-layouts, run_spans(): lax.scan(advance, memory, (shaped(queries), shaped(keys_in), shaped(value...  8.24 us
    dot_general x4, matrix products, attend_block(): jnp.einsum('hrp,pd->hrd', expos.astype(jnp.bfloat16), block_values, prefe...  5.88 us
    unnamed x46, local copies, waits for them, and re-layouts  5.65 us
    ppermute x4, starting transfers between devices, from_behind(): lax.ppermute(value, axis, [(source, source + steps) for source in range(i...  5.13 us
    dot_general x4, matrix products, attend_block(): jnp.einsum('rhd,pd->hrp', query_rot, block_keys, preferred_element_type=j...  5.1 us
  transfers between devices with their start and end apart: 5, of which 4 were waited for; matrix products, arithmetic and copies ran while one was open for 59% of the time, Pallas kernels for 0%

commit v1 on v0

v1 whole, which is shorter than its diff:
```python
import functools

import jax
import jax.numpy as jnp
import numpy as np
from jax import lax
from jax.experimental import pallas as pl
from jax.experimental.pallas import tpu as pltpu
from jax.sharding import PartitionSpec as P

D_K = 128
D_V = 128
K_HEADS = 16
VALUE_HEAD_COUNT = 32
CONV = 4
Q_HEADS = 16
KV_HEADS = 2
HEAD_DIM = 256
ROPE_THETA = 10000000.0
REPEATS = VALUE_HEAD_COUNT // K_HEADS
RIM = 16

HIGHEST = lax.Precision.HIGHEST
MESH = pl.DeviceIdType.MESH
F32 = jnp.float32
BF16 = jnp.bfloat16


def mm(left, right):
    return jnp.dot(left.astype(BF16), right.astype(BF16), preferred_element_type=F32)


def mmt(left, right):
    return lax.dot_general(
        left.astype(BF16),
        right.astype(BF16),
        (((1,), (1,)), ((), ())),
        preferred_element_type=F32,
    )


def sigmoid(x):
    return 1.0 / (1.0 + jnp.exp(-x))


def unit_rows(x):
    return x * lax.rsqrt(jnp.sum(x * x, -1, keepdims=True) + 1e-06)


def iotas(rows):
    row = lax.broadcasted_iota(jnp.int32, (rows, rows), 0)
    col = lax.broadcasted_iota(jnp.int32, (rows, rows), 1)
    return row, col


def delta_local(gram, scores, key, key_t, query, value, cum, cum_row, beta):
    rows = gram.shape[0]
    row, col = iotas(rows)
    lower = row >= col
    within = jnp.where(lower, jnp.exp(jnp.where(lower, cum - cum_row, 0.0)), 0.0)
    coupling = jnp.where(row > col, beta * gram * within, 0.0).astype(BF16)
    zero = jnp.zeros_like(coupling)
    same16 = (row // 16) == (col // 16)
    same64 = (row // 64) == (col // 64)

    power = jnp.where(same16, -coupling, zero)
    extra = power.astype(F32)
    for _ in range(3):
        power = mm(power, power).astype(BF16)
        extra = extra + power.astype(F32) + mm(extra, power)

    rest = jnp.where(same64 & ~same16, coupling, zero)
    step = -(rest.astype(F32) + mm(extra, rest))
    step2 = mm(step, step)
    grow = step + step2 + mm(step, step2)
    extra = extra + grow + mm(grow, extra)

    rest = jnp.where(same64, zero, coupling)
    step = (-(rest.astype(F32) + mm(extra, rest))).astype(BF16)
    step2 = mm(step, step)
    decay_now = jnp.exp(cum)
    right = jnp.concatenate([beta * value, (beta * decay_now) * key], -1)
    solved = right + mm(extra, right)
    solved = solved + mm(step2, solved)
    solved = (solved + mm(step, solved)).astype(BF16)

    inner = (scores * within).astype(BF16)
    both = mm(inner, solved)
    out_local = both[:, :D_V]
    state_query = query * decay_now - both[:, D_V:]
    last = cum[rows - 1 :, :]
    ended = mm(key_t * jnp.exp(last - cum_row), solved)
    offset = ended[:, :D_V]
    krow, kcol = iotas(D_K)
    transfer = jnp.where(krow == kcol, jnp.exp(last), 0.0) - ended[:, D_V:]
    return out_local, state_query, offset, transfer


def rope_norm(x, gain, cosine, sine):
    normed = x * lax.rsqrt(jnp.mean(x * x, -1, keepdims=True) + 1e-06) * gain
    half = HEAD_DIM // 8
    front = normed[:, :128]
    lane = lax.broadcasted_iota(jnp.int32, front.shape, 1)
    partner = jnp.where(lane < half, pltpu.roll(front, 128 - half, 1), pltpu.roll(front, half, 1))
    front = front * cosine + partner * sine
    return jnp.concatenate([front, normed[:, 128:]], -1).astype(BF16)


def kernel(n, *refs):
    ins = refs[:18]
    (
        qraw_h, kraw_h, vraw_h, ogate_h, cq_h, ck_h, cv_h, decay_h, beta_h, ngain_h,
        qh_h, gh_h, kh_h, vh_h, qgain_h, kgain_h, cos_h, sin_h,
    ) = ins
    dn_out, at_out = refs[18:20]
    (
        qraw, kraw, vraw, ogate, cq, ck, cv, decay, beta_in, ngain,
        qh, gh, kh, qgain, kgain, cosine, sine,
        rim_q, rim_k, rim_v, pad, cum_s, cumt_s,
        out_local_s, state_query_s, offset_s, transfer_s,
        kbuf, vbuf, qrot, m_s, l_s, acc_s, in_buf, send_buf, dn_v, at_v,
        load_sem, rim_send, rim_recv, kv_send, kv_recv, st_send, st_recv, out_sem,
    ) = refs[20:]
    rows = qraw.shape[0]
    me = lax.axis_index("ctx")
    head = lax.axis_index("head")
    later = jnp.minimum(me + 1, n - 1)
    behind = jnp.maximum(me - 1, 0)
    key_heads = qraw.shape[1] // D_K
    value_heads = vraw.shape[1] // D_V
    q_heads = qh.shape[1] // HEAD_DIM
    kv_index = head * q_heads // (Q_HEADS // KV_HEADS)
    kv_cols = pl.ds(pl.multiple_of(kv_index * HEAD_DIM, HEAD_DIM), HEAD_DIM)
    own_rows = pl.ds(pl.multiple_of(me * rows, rows), rows)

    barrier = pltpu.get_barrier_semaphore()

    @pl.loop(1, n)
    def _(d):
        pl.semaphore_signal(
            barrier, inc=1, device_id={"ctx": lax.rem(me + d, n)}, device_id_type=MESH
        )

    pairs = [
        (kh_h.at[:, kv_cols], kh),
        (cos_h.at[own_rows], cosine),
        (sin_h.at[own_rows], sine),
        (kgain_h, kgain),
        (vh_h.at[:, kv_cols], vbuf.at[me]),
        (qraw_h, qraw),
        (kraw_h, kraw),
        (vraw_h, vraw),
        (decay_h, decay),
        (beta_h, beta_in),
        (cq_h, cq),
        (ck_h, ck),
        (cv_h, cv),
        (ngain_h, ngain),
        (qgain_h, qgain),
        (qh_h, qh),
        (gh_h, gh),
        (ogate_h, ogate),
    ]
    loads = [
        pltpu.make_async_copy(source, target, load_sem.at[i])
        for i, (source, target) in enumerate(pairs)
    ]
    for load in loads:
        load.start()

    for load in loads[:5]:
        load.wait()
    kbuf[me] = rope_norm(kh[...].astype(F32), kgain[...], cosine[...], sine[...])
    for load in loads[5:15]:
        load.wait()
    pl.semaphore_wait(barrier, n - 1)

    def rim_copy(raw, rim, i, dest):
        return pltpu.make_async_remote_copy(
            src_ref=raw.at[pl.ds(rows - RIM, RIM)],
            dst_ref=rim,
            send_sem=rim_send.at[i],
            recv_sem=rim_recv.at[i],
            device_id={"ctx": dest},
            device_id_type=MESH,
        )

    def kv_copy(buf, i, block, dest):
        return pltpu.make_async_remote_copy(
            src_ref=buf.at[block],
            dst_ref=buf.at[block],
            send_sem=kv_send.at[i, dest],
            recv_sem=kv_recv.at[i, block],
            device_id={"ctx": dest},
            device_id_type=MESH,
        )

    def state_copy(h, dest):
        return pltpu.make_async_remote_copy(
            src_ref=send_buf.at[h],
            dst_ref=in_buf.at[h],
            send_sem=st_send.at[h],
            recv_sem=st_recv.at[h],
            device_id={"ctx": dest},
            device_id_type=MESH,
        )

    rims = [(qraw, rim_q), (kraw, rim_k), (vraw, rim_v)]

    @pl.when(me < n - 1)
    def _():
        for i, (raw, rim) in enumerate(rims):
            rim_copy(raw, rim, i, later).start()

    @pl.loop(me + 1, n)
    def _(dest):
        kv_copy(kbuf, 0, me, dest).start()
        kv_copy(vbuf, 1, me, dest).start()

    row, col = iotas(rows)
    ones_low = jnp.where(row >= col, 1.0, 0.0)
    cum_s[...] = jnp.dot(ones_low, decay[...], precision=HIGHEST, preferred_element_type=F32)
    ones_up = jnp.where(row <= col, 1.0, 0.0)
    cumt_s[...] = lax.dot_general(
        decay[...], ones_up, (((0,), (0,)), ((), ())), precision=HIGHEST,
        preferred_element_type=F32,
    )

    @pl.when(me == 0)
    def _():
        for _, rim in rims:
            rim[...] = jnp.zeros_like(rim)
        in_buf[...] = jnp.zeros_like(in_buf)

    @pl.when(me > 0)
    def _():
        for i, (raw, rim) in enumerate(rims):
            rim_copy(raw, rim, i, behind).wait_recv()

    def conv_silu(slot, raw, rim, taps, cols):
        pad[slot, 0:RIM] = rim[:, cols].astype(F32)
        pad[slot, RIM : RIM + rows] = raw[:, cols].astype(F32)
        weights = taps[:, cols]
        total = None
        for j in range(CONV):
            first = RIM - (CONV - 1) + j
            term = weights[j : j + 1] * pad[slot, first : first + rows]
            total = term if total is None else total + term
        return total * sigmoid(total)

    def head_pair(kh_i, carry):
        cols = pl.ds(pl.multiple_of(kh_i * D_K, D_K), D_K)
        query = unit_rows(conv_silu(0, qraw, rim_q, cq, cols)) * D_K ** (-0.5)
        key = unit_rows(conv_silu(1, kraw, rim_k, ck, cols))
        key_t = key.T
        gram = mm(key, key_t)
        scores = mm(query, key_t)
        lane = lax.broadcasted_iota(jnp.int32, (rows, value_heads), 1)
        for r in range(REPEATS):
            h = kh_i * REPEATS + r
            vcols = pl.ds(pl.multiple_of(h * D_V, D_V), D_V)
            value = conv_silu(2 + r, vraw, rim_v, cv, vcols)
            cum = jnp.sum(jnp.where(lane == h, cum_s[...], 0.0), -1, keepdims=True)
            beta = jnp.sum(jnp.where(lane == h, beta_in[...], 0.0), -1, keepdims=True)
            out_local, state_query, offset, transfer = delta_local(
                gram, scores, key, key_t, query, value, cum, cumt_s[pl.ds(h, 1), :], beta
            )
            out_local_s[:, vcols] = out_local
            state_query_s[:, vcols] = state_query.astype(BF16)
            offset_s[h] = offset
            transfer_s[h] = transfer.astype(BF16)
            send_buf[h] = offset.astype(BF16)

        @pl.when(me == 0)
        def _():
            for r in range(REPEATS):
                state_copy(kh_i * REPEATS + r, later).start()

        return carry

    lax.fori_loop(0, key_heads, head_pair, 0)

    for load in loads[15:]:
        load.wait()

    for i in range(q_heads):
        cols = slice(i * HEAD_DIM, (i + 1) * HEAD_DIM)
        qrot[i] = rope_norm(qh[:, cols].astype(F32), qgain[...], cosine[...], sine[...])

    def relay():
        @pl.loop(0, value_heads)
        def _(h):
            state_copy(h, behind).wait_recv()

            @pl.when(me < n - 1)
            def _():
                send_buf[h] = (mm(transfer_s[h], in_buf[h]) + offset_s[h]).astype(BF16)
                state_copy(h, later).start()

    scale = HEAD_DIM ** (-0.5)

    def attend(i, block, diagonal):
        scores = mmt(qrot[i], kbuf[block]) * scale
        if diagonal:
            arow, acol = iotas(rows)
            scores = jnp.where(acol <= arow, scores, -1e30)
        top = jnp.max(scores, -1, keepdims=True)
        if diagonal:
            new = top
        else:
            old = m_s[i]
            new = jnp.maximum(old, top)
        expos = jnp.exp(scores - new)
        total = jnp.sum(expos, -1, keepdims=True)
        mixed = mm(expos, vbuf[block])
        if not diagonal:
            factor = jnp.exp(old - new)
            total = total + l_s[i] * factor
            mixed = mixed + acc_s[i] * factor
        m_s[i] = new
        l_s[i] = total
        acc_s[i] = mixed

    for i in range(q_heads):
        attend(i, me, True)

    @pl.when(me == 1)
    def _():
        relay()

    @pl.loop(0, me)
    def _(block):
        kv_copy(kbuf, 0, block, behind).wait_recv()
        kv_copy(vbuf, 1, block, behind).wait_recv()
        for i in range(q_heads):
            attend(i, block, False)

    for i in range(q_heads):
        cols = slice(i * HEAD_DIM, (i + 1) * HEAD_DIM)
        gate = sigmoid(gh[:, cols].astype(F32))
        at_v[:, cols] = (acc_s[i] / l_s[i] * gate).astype(BF16)
    at_copy = pltpu.make_async_copy(at_v, at_out, out_sem.at[0])
    at_copy.start()

    @pl.when(me > 1)
    def _():
        relay()

    gain = ngain[...]

    @pl.loop(0, value_heads)
    def _(h):
        vcols = pl.ds(pl.multiple_of(h * D_V, D_V), D_V)
        out = out_local_s[:, vcols] + mm(state_query_s[:, vcols], in_buf[h])
        normed = out * lax.rsqrt(jnp.mean(out * out, -1, keepdims=True) + 1e-06) * gain
        gate = ogate[:, vcols].astype(F32)
        dn_v[:, vcols] = (normed * (gate * sigmoid(gate))).astype(BF16)

    dn_copy = pltpu.make_async_copy(dn_v, dn_out, out_sem.at[1])
    dn_copy.start()

    @pl.when(me < n - 1)
    def _():
        for i, (raw, rim) in enumerate(rims):
            rim_copy(raw, rim, i, later).wait_send()

        @pl.loop(0, value_heads)
        def _(h):
            state_copy(h, later).wait_send()

    @pl.loop(me + 1, n)
    def _(dest):
        kv_copy(kbuf, 0, me, dest).wait_send()
        kv_copy(vbuf, 1, me, dest).wait_send()

    at_copy.wait()
    dn_copy.wait()


def rope_tables(count):
    half = HEAD_DIM // 8
    frequency = (ROPE_THETA ** (-np.arange(half, dtype=np.float64) / half)).astype(np.float32)
    angles = np.arange(count, dtype=np.float32)[:, None] * frequency[None, :]
    cosine = np.cos(angles.astype(np.float64)).astype(np.float32)
    sine = np.sin(angles.astype(np.float64)).astype(np.float32)
    one = np.ones((count, 128 - 2 * half), np.float32)
    return (
        np.concatenate([cosine, cosine, one], 1),
        np.concatenate([-sine, sine, 0 * one], 1),
    )


def body(
    query_raw, key_raw, value_raw, out_gate, conv_query, conv_key, conv_value, decay_log,
    write_beta, norm_gain, query_heads, gate_heads, key_heads, value_heads, query_gain, key_gain,
):
    n = lax.axis_size("ctx")
    rows = query_raw.shape[0]
    value_count = value_raw.shape[1] // D_V
    q_count = query_heads.shape[1] // HEAD_DIM
    cosine, sine = rope_tables(n * rows)
    ins = (
        query_raw, key_raw, value_raw, out_gate, conv_query, conv_key, conv_value, decay_log,
        write_beta, norm_gain[None], query_heads, gate_heads, key_heads, value_heads,
        query_gain[None], key_gain[None], jnp.asarray(cosine), jnp.asarray(sine),
    )
    like = lambda array: pltpu.VMEM(array.shape, array.dtype)
    scratch = [like(a) for a in ins[:12]]
    scratch += [pltpu.VMEM((rows, HEAD_DIM), BF16), like(ins[14]), like(ins[15])]
    scratch += [pltpu.VMEM((rows, 128), F32)] * 2
    scratch += [pltpu.VMEM((RIM, a.shape[1]), BF16) for a in ins[:3]]
    scratch += [
        pltpu.VMEM((2 + REPEATS, RIM + rows, 128), F32),
        pltpu.VMEM((rows, value_count), F32),
        pltpu.VMEM((value_count, rows), F32),
        pltpu.VMEM((rows, value_count * D_V), F32),
        pltpu.VMEM((rows, value_count * D_K), BF16),
        pltpu.VMEM((value_count, D_K, D_V), F32),
        pltpu.VMEM((value_count, D_K, D_K), BF16),
        pltpu.VMEM((n, rows, HEAD_DIM), BF16),
        pltpu.VMEM((n, rows, HEAD_DIM), BF16),
        pltpu.VMEM((q_count, rows, HEAD_DIM), BF16),
        pltpu.VMEM((q_count, rows, 1), F32),
        pltpu.VMEM((q_count, rows, 1), F32),
        pltpu.VMEM((q_count, rows, HEAD_DIM), F32),
        pltpu.VMEM((value_count, D_K, D_V), BF16),
        pltpu.VMEM((value_count, D_K, D_V), BF16),
        like(out_gate),
        like(gate_heads),
        pltpu.SemaphoreType.DMA((18,)),
        pltpu.SemaphoreType.DMA((3,)),
        pltpu.SemaphoreType.DMA((3,)),
        pltpu.SemaphoreType.DMA((2, n)),
        pltpu.SemaphoreType.DMA((2, n)),
        pltpu.SemaphoreType.DMA((value_count,)),
        pltpu.SemaphoreType.DMA((value_count,)),
        pltpu.SemaphoreType.DMA((2,)),
    ]
    return pl.pallas_call(
        functools.partial(kernel, n),
        out_shape=(
            jax.ShapeDtypeStruct(out_gate.shape, BF16),
            jax.ShapeDtypeStruct(gate_heads.shape, BF16),
        ),
        in_specs=[pl.BlockSpec(memory_space=pl.ANY)] * 18,
        out_specs=(pl.BlockSpec(memory_space=pl.ANY),) * 2,
        scratch_shapes=scratch,
        compiler_params=pltpu.CompilerParams(
            collective_id=0, has_side_effects=True, vmem_limit_bytes=48 * 2**20
        ),
        name="token_mixing",
    )(*ins)


def solution(mesh):
    tokens = P(("grp", "ctx"), "head")
    taps = P(None, "head")
    shared = P(("grp", "ctx"), None)
    placed = (
        tokens, tokens, tokens, tokens, taps, taps, taps, tokens, tokens, P(),
        tokens, tokens, shared, shared, P(), P(),
    )
    return jax.shard_map(
        body, mesh=mesh, in_specs=placed, out_specs=(tokens, tokens), check_vma=False
    )
```

time: 178 us -> 55.1 us (0.31); the launches traced: 175 us -> 54.5 us
  matrix products: 84.6 us -> 0 us
  Pallas kernels: 0 us -> 39.9 us
  waiting for transfers between devices: 24.4 us -> 0 us
  other arithmetic: 16.5 us -> 0 us
  between operations: 14.7 us -> 0.75 us
  local copies, waits for them, and re-layouts: 25.4 us -> 13.8 us
  starting transfers between devices: 5.17 us -> 0 us
  loops' own time: 4.5 us -> 0 us
    dot_general x143 -> x0, matrix products: 84.6 us -> none  [the longest x135 73.6 us: matmul_heads(): return jnp.einsum('hij,hjk->hik', left, right, precision=HIGHEST)]
    pallas_call x0 -> x1, Pallas kernels: none -> 39.9 us  [body(): pl.pallas_call(functools.partial(kernel, n), out_shape=(jax.ShapeDtypeStr...]
    ppermute x4 -> x0, waiting for transfers between devices: 24.4 us -> none  [from_behind(): lax.ppermute(value, axis, [(source, source + steps) for source in range(i...]
    dynamic_slice x12 -> x0, local copies, waits for them, and re-layouts: 10.6 us -> none  [the longest x8 8.24 us: run_spans(): lax.scan(advance, memory, (shaped(queries), shaped(keys_in), shaped(value...]
    unnamed x46 -> x36, local copies, waits for them, and re-layouts: 5.65 us -> 13.8 us
    ppermute x4 -> x0, starting transfers between devices: 5.13 us -> none  [from_behind(): lax.ppermute(value, axis, [(source, source + steps) for source in range(i...]
    another operation x4 -> x0, loops' own time: 4.5 us -> none  [the longest x1 2.92 us: body(): lax.scan(one_block, running, jnp.arange(block_count, dtype=jnp.int32))]
    mul x14 -> x0, other arithmetic: 4.02 us -> none  [the longest x1 1.46 us: delta_inputs(): queries = unit_rows(query_conv.reshape(row_count, -1, D_K)) * D_K ** (-0.5)]
  transfers between devices with their start and end apart: 5 -> 0, of which waited for: 4 -> 0; matrix products, arithmetic and copies ran while one was open for 59% -> 0% of each run, Pallas kernels for 0% -> 0%
where the time goes in v1:
time: 55.1 us; the launch traced here: 54.5 us
  Pallas kernels  39.9 us (72%)
  local copies, waits for them, and re-layouts  13.8 us (25%)
  between operations  0.75 us (1%)
    pallas_call x1, Pallas kernels, body(): pl.pallas_call(functools.partial(kernel, n), out_shape=(jax.ShapeDtypeStr...  39.9 us
    unnamed x36, local copies, waits for them, and re-layouts  13.8 us

profile of v1, /device:TPU:24, one launch (start us, length us, event | category | flops | bytes accessed | tf_op | source)
XLA Modules:
  0.0 54.5 jit_solution(295834444451265052)
XLA Ops:
  0.6 0.0 copy-start.6
  0.6 0.9 %copy.20.refs_7_ = f32[256,8]{1,0:T(8,128)S(1)} copy(f32[256,8]{0,1:T(8,128)} %param.25) | data formatting | bytes 16384 | tf_op args[7]
  1.5 0.0 copy-start.10
  1.5 0.0 copy-start.13
  1.5 0.0 copy-start.14
  1.5 0.0 copy-start.15
  1.6 0.8 %copy.21.refs_8_ = f32[256,8]{1,0:T(8,128)S(1)} copy(f32[256,8]{0,1:T(8,128)} %param.26) | data formatting | bytes 16384 | tf_op args[8]
  2.4 0.0 copy-done.6
  2.4 0.0 copy-done.10
  2.5 0.0 copy-start
  2.5 1.0 %copy-done = bf16[256,1024]{1,0:T(8,128)(2,1)S(1)} copy-done((bf16[256,1024]{1,0:T(8,128)(2,1)S(1)}, bf16[256,1024]{1,0:T(8,128)(2,1)}, u32[]{:S(2)}) %copy-start) | copy-done | bytes 524312
  3.5 1.0 %copy-done.1 = bf16[256,1024]{1,0:T(8,128)(2,1)S(1)} copy-done((bf16[256,1024]{1,0:T(8,128)(2,1)S(1)}, bf16[256,1024]{1,0:T(8,128)(2,1)}, u32[]{:S(2)}) %copy-start.1) | copy-done | bytes 524312
  4.5 1.0 %copy-done.2 = bf16[256,1024]{1,0:T(8,128)(2,1)S(1)} copy-done((bf16[256,1024]{1,0:T(8,128)(2,1)S(1)}, bf16[256,1024]{1,0:T(8,128)(2,1)}, u32[]{:S(2)}) %copy-start.2) | copy-done | bytes 524312
  5.6 1.0 %copy-done.3 = bf16[256,1024]{1,0:T(8,128)(2,1)S(1)} copy-done((bf16[256,1024]{1,0:T(8,128)(2,1)S(1)}, bf16[256,1024]{1,0:T(8,128)(2,1)}, u32[]{:S(2)}) %copy-start.3) | copy-done | bytes 524312
  6.6 1.0 %copy-done.4 = f32[1024,128]{1,0:T(8,128)S(1)} copy-done((f32[1024,128]{1,0:T(8,128)S(1)}, f32[1024,128]{1,0:T(8,128)}, u32[]{:S(2)}) %copy-start.4) | copy-done | bytes 524312
  7.7 1.0 %copy-done.5 = f32[1024,128]{1,0:T(8,128)S(1)} copy-done((f32[1024,128]{1,0:T(8,128)S(1)}, f32[1024,128]{1,0:T(8,128)}, u32[]{:S(2)}) %copy-start.5) | copy-done | bytes 524312
  8.7 0.9 %copy-done.7 = bf16[256,512]{1,0:T(8,128)(2,1)S(1)} copy-done((bf16[256,512]{1,0:T(8,128)(2,1)S(1)}, bf16[256,512]{1,0:T(8,128)(2,1)}, u32[]{:S(2)}) %copy-start.7) | copy-done | bytes 262168
  9.7 0.9 %copy-done.8 = bf16[256,512]{1,0:T(8,128)(2,1)S(1)} copy-done((bf16[256,512]{1,0:T(8,128)(2,1)S(1)}, bf16[256,512]{1,0:T(8,128)(2,1)}, u32[]{:S(2)}) %copy-start.8) | copy-done | bytes 262168
  10.6 0.9 %copy-done.9 = bf16[256,512]{1,0:T(8,128)(2,1)S(1)} copy-done((bf16[256,512]{1,0:T(8,128)(2,1)S(1)}, bf16[256,512]{1,0:T(8,128)(2,1)}, u32[]{:S(2)}) %copy-start.9) | copy-done | bytes 262168
  11.6 0.7 %copy-done.11 = f32[4,512]{1,0:T(4,128)S(1)} copy-done((f32[4,512]{1,0:T(4,128)S(1)}, f32[4,512]{1,0:T(4,128)}, u32[]{:S(2)}) %copy-start.11) | copy-done | bytes 8216
  12.3 0.7 %copy-done.12 = f32[4,512]{1,0:T(4,128)S(1)} copy-done((f32[4,512]{1,0:T(4,128)S(1)}, f32[4,512]{1,0:T(4,128)}, u32[]{:S(2)}) %copy-start.12) | copy-done | bytes 8216
  13.0 39.9 %token_mixing.1 = (bf16[256,1024]{1,0:T(8,128)(2,1)S(1)}, bf16[256,1024]{1,0:T(8,128)(2,1)S(1)}) custom-call(bf16[256,512]{1,0:T(8,128)(2,1)S(1)} %copy-done.6, bf16[256,512]{1,0:T(8,128)(2,1)S(1)} %copy-done.7, bf16[256,1024]{1,0:T(8,128)(2,1)S(1)} %copy-done, bf16[256,1024]{1,0:T(8,128)(2,1)S(1)} %copy-done.1, f32[4,512]{1,0:T(4,128)S(1)} %copy-done.11, ...), custom_call_target="tpu_custom_call" | custom-call | tf_op jit(solution)/shard_map/token_mixing/pallas_call | solution.py:439
  52.9 0.8 %copy.24 = bf16[256,1024]{1,0:T(8,128)(2,1)} copy(bf16[256,1024]{1,0:T(8,128)(2,1)S(1)} %get-tuple-element.4) | data formatting | bytes 1048576
  53.7 0.8 %copy.25 = bf16[256,1024]{1,0:T(8,128)(2,1)} copy(bf16[256,1024]{1,0:T(8,128)(2,1)S(1)} %get-tuple-element.5) | data formatting | bytes 1048576
  (13 shorter events, 0.0 us)
Async XLA Ops:
  0.6 1.8 %copy-start.6 = (bf16[256,512]{1,0:T(8,128)(2,1)S(1)}, bf16[256,512]{1,0:T(8,128)(2,1)}, u32[]{:S(2)}) copy-start(bf16[256,512]{1,0:T(8,128)(2,1)} %refs_0_.1) | copy-start | bytes 786436
  1.5 0.9 %copy-start.10 = (f32[4,1024]{1,0:T(4,128)S(1)}, f32[4,1024]{1,0:T(4,128)}, u32[]{:S(2)}) copy-start(f32[4,1024]{1,0:T(4,128)} %refs_6_.1) | copy-start | bytes 49156
  1.5 0.9 %copy-start.13 = (f32[256]{0:T(256)S(1)}, f32[256]{0:T(256)}, u32[]{:S(2)}) copy-start(f32[256]{0:T(256)} %param.32) | copy-start | bytes 3076
  1.5 0.9 %copy-start.14 = (f32[256]{0:T(256)S(1)}, f32[256]{0:T(256)}, u32[]{:S(2)}) copy-start(f32[256]{0:T(256)} %param.33) | copy-start | bytes 3076
  1.5 0.9 %copy-start.15 = (f32[128]{0:T(128)S(1)}, f32[128]{0:T(128)}, u32[]{:S(2)}) copy-start(f32[128]{0:T(128)} %param.27) | copy-start | bytes 1540
  2.5 1.0 %copy-start = (bf16[256,1024]{1,0:T(8,128)(2,1)S(1)}, bf16[256,1024]{1,0:T(8,128)(2,1)}, u32[]{:S(2)}) copy-start(bf16[256,1024]{1,0:T(8,128)(2,1)} %refs_2_.1) | copy-start | bytes 1572868
  3.5 1.0 %copy-start.1 = (bf16[256,1024]{1,0:T(8,128)(2,1)S(1)}, bf16[256,1024]{1,0:T(8,128)(2,1)}, u32[]{:S(2)}) copy-start(bf16[256,1024]{1,0:T(8,128)(2,1)} %refs_3_.1) | copy-start | bytes 1572868
  4.5 1.0 %copy-start.2 = (bf16[256,1024]{1,0:T(8,128)(2,1)S(1)}, bf16[256,1024]{1,0:T(8,128)(2,1)}, u32[]{:S(2)}) copy-start(bf16[256,1024]{1,0:T(8,128)(2,1)} %refs_10_.1) | copy-start | bytes 1572868
  5.6 1.0 %copy-start.3 = (bf16[256,1024]{1,0:T(8,128)(2,1)S(1)}, bf16[256,1024]{1,0:T(8,128)(2,1)}, u32[]{:S(2)}) copy-start(bf16[256,1024]{1,0:T(8,128)(2,1)} %refs_11_.1) | copy-start | bytes 1572868
  6.6 1.0 %copy-start.4 = (f32[1024,128]{1,0:T(8,128)S(1)}, f32[1024,128]{1,0:T(8,128)}, u32[]{:S(2)}) copy-start(f32[1024,128]{1,0:T(8,128)} %constant.5.clone.refs_17_) | copy-start | bytes 1572868
  7.7 1.0 %copy-start.5 = (f32[1024,128]{1,0:T(8,128)S(1)}, f32[1024,128]{1,0:T(8,128)}, u32[]{:S(2)}) copy-start(f32[1024,128]{1,0:T(8,128)} %constant.4.clone.refs_16_) | copy-start | bytes 1572868
  8.7 0.9 %copy-start.7 = (bf16[256,512]{1,0:T(8,128)(2,1)S(1)}, bf16[256,512]{1,0:T(8,128)(2,1)}, u32[]{:S(2)}) copy-start(bf16[256,512]{1,0:T(8,128)(2,1)} %refs_1_.1) | copy-start | bytes 786436
  9.7 0.9 %copy-start.8 = (bf16[256,512]{1,0:T(8,128)(2,1)S(1)}, bf16[256,512]{1,0:T(8,128)(2,1)}, u32[]{:S(2)}) copy-start(bf16[256,512]{1,0:T(8,128)(2,1)} %refs_12_.1) | copy-start | bytes 786436
  10.6 0.9 %copy-start.9 = (bf16[256,512]{1,0:T(8,128)(2,1)S(1)}, bf16[256,512]{1,0:T(8,128)(2,1)}, u32[]{:S(2)}) copy-start(bf16[256,512]{1,0:T(8,128)(2,1)} %refs_13_.1) | copy-start | bytes 786436
  11.6 0.7 %copy-start.11 = (f32[4,512]{1,0:T(4,128)S(1)}, f32[4,512]{1,0:T(4,128)}, u32[]{:S(2)}) copy-start(f32[4,512]{1,0:T(4,128)} %refs_4_.1) | copy-start | bytes 24580
  12.3 0.7 %copy-start.12 = (f32[4,512]{1,0:T(4,128)S(1)}, f32[4,512]{1,0:T(4,128)}, u32[]{:S(2)}) copy-start(f32[4,512]{1,0:T(4,128)} %refs_5_.1) | copy-start | bytes 24580

commit v2 on v1

--- a/solution.py
+++ b/solution.py
@@ -53,47 +53,62 @@
     return row, col
 
 
-def delta_local(gram, scores, key, key_t, query, value, cum, cum_row, beta):
-    rows = gram.shape[0]
-    row, col = iotas(rows)
-    lower = row >= col
-    within = jnp.where(lower, jnp.exp(jnp.where(lower, cum - cum_row, 0.0)), 0.0)
-    coupling = jnp.where(row > col, beta * gram * within, 0.0).astype(BF16)
-    zero = jnp.zeros_like(coupling)
-    same16 = (row // 16) == (col // 16)
-    same64 = (row // 64) == (col // 64)
-
-    power = jnp.where(same16, -coupling, zero)
-    extra = power.astype(F32)
+def delta_local(heads, masks):
+    lower, strict, eye, same16, same64 = masks
+    identity = jnp.where(eye, 1.0, 0.0)
+    withins = [
+        jnp.where(lower, jnp.exp(jnp.where(lower, h["cum"] - h["cum_row"], 0.0)), 0.0)
+        for h in heads
+    ]
+    couplings = [
+        jnp.where(strict, h["beta"] * h["gram"] * within, 0.0)
+        for h, within in zip(heads, withins)
+    ]
+    inners = [(h["scores"] * within).astype(BF16) for h, within in zip(heads, withins)]
+    rest16 = [jnp.where(same64 & ~same16, c, 0.0).astype(BF16) for c in couplings]
+    rest64 = [jnp.where(same64, 0.0, c).astype(BF16) for c in couplings]
+
+    powers = [jnp.where(same16, -c, 0.0) for c in couplings]
+    inverses = [(identity + p).astype(BF16) for p in powers]
+    powers = [p.astype(BF16) for p in powers]
     for _ in range(3):
-        power = mm(power, power).astype(BF16)
-        extra = extra + power.astype(F32) + mm(extra, power)
-
-    rest = jnp.where(same64 & ~same16, coupling, zero)
-    step = -(rest.astype(F32) + mm(extra, rest))
-    step2 = mm(step, step)
-    grow = step + step2 + mm(step, step2)
-    extra = extra + grow + mm(grow, extra)
-
-    rest = jnp.where(same64, zero, coupling)
-    step = (-(rest.astype(F32) + mm(extra, rest))).astype(BF16)
-    step2 = mm(step, step)
-    decay_now = jnp.exp(cum)
-    right = jnp.concatenate([beta * value, (beta * decay_now) * key], -1)
-    solved = right + mm(extra, right)
-    solved = solved + mm(step2, solved)
-    solved = (solved + mm(step, solved)).astype(BF16)
-
-    inner = (scores * within).astype(BF16)
-    both = mm(inner, solved)
-    out_local = both[:, :D_V]
-    state_query = query * decay_now - both[:, D_V:]
-    last = cum[rows - 1 :, :]
-    ended = mm(key_t * jnp.exp(last - cum_row), solved)
-    offset = ended[:, :D_V]
+        squares = [mm(p, p) for p in powers]
+        factors = [(identity + p).astype(BF16) for p in squares]
+        powers = [p.astype(BF16) for p in squares]
+        inverses = [mm(i, f).astype(BF16) for i, f in zip(inverses, factors)]
+
+    steps = [-mm(i, r) for i, r in zip(inverses, rest16)]
+    seconds = [mm(p, p) for p in steps]
+    grows = [
+        mm(identity + p, identity + p2).astype(BF16) for p, p2 in zip(steps, seconds)
+    ]
+    inverses = [mm(g, i).astype(BF16) for g, i in zip(grows, inverses)]
+
+    steps = [(-mm(i, r)).astype(BF16) for i, r in zip(inverses, rest64)]
+    seconds = [mm(p, p).astype(BF16) for p in steps]
+    decays = [jnp.exp(h["cum"]) for h in heads]
+    rights = [
+        jnp.concatenate([h["beta"] * h["value"], (h["beta"] * d) * h["key"]], -1)
+        for h, d in zip(heads, decays)
+    ]
+    solved = [mm(i, r) for i, r in zip(inverses, rights)]
+    solved = [x + mm(p, x) for x, p in zip(solved, seconds)]
+    solved = [(x + mm(p, x)).astype(BF16) for x, p in zip(solved, steps)]
+
+    lasts = [h["cum"][h["cum"].shape[0] - 1 :, :] for h in heads]
+    ended = [
+        mm(h["key_t"] * jnp.exp(last - h["cum_row"]), x)
+        for h, last, x in zip(heads, lasts, solved)
+    ]
+    boths = [mm(inner, x) for inner, x in zip(inners, solved)]
     krow, kcol = iotas(D_K)
-    transfer = jnp.where(krow == kcol, jnp.exp(last), 0.0) - ended[:, D_V:]
-    return out_local, state_query, offset, transfer
+    results = []
+    for h, d, last, end, both in zip(heads, decays, lasts, ended, boths):
+        transfer = jnp.where(krow == kcol, jnp.exp(last), 0.0) - end[:, D_V:]
+        results.append(
+            (both[:, :D_V], h["query"] * d - both[:, D_V:], end[:, :D_V], transfer)
+        )
+    return results
 
 
 def rope_norm(x, gain, cosine, sine):
@@ -116,16 +131,18 @@
     (
         qraw, kraw, vraw, ogate, cq, ck, cv, decay, beta_in, ngain,
         qh, gh, kh, qgain, kgain, cosine, sine,
-        rim_q, rim_k, rim_v, pad, cum_s, cumt_s,
+        rim_q, rim_k, rim_v, pad, cum_s, beta_s, cumt_s,
         out_local_s, state_query_s, offset_s, transfer_s,
-        kbuf, vbuf, qrot, m_s, l_s, acc_s, in_buf, send_buf, dn_v, at_v,
-        load_sem, rim_send, rim_recv, kv_send, kv_recv, st_send, st_recv, out_sem,
+        kv, qrot, m_s, l_s, acc_s, in_buf, send_buf, dn_v, at_v,
+        load_sem, rim_send, rim_recv, kv_send, kv_recv, pass_send, pass_recv, st_send, st_recv, out_sem,
     ) = refs[20:]
     rows = qraw.shape[0]
     me = lax.axis_index("ctx")
     head = lax.axis_index("head")
     later = jnp.minimum(me + 1, n - 1)
     behind = jnp.maximum(me - 1, 0)
+    core = lax.rem(head, 2)
+    peer = head + 1 - 2 * core
     key_heads = qraw.shape[1] // D_K
     value_heads = vraw.shape[1] // D_V
     q_heads = qh.shape[1] // HEAD_DIM
@@ -141,12 +158,14 @@
             barrier, inc=1, device_id={"ctx": lax.rem(me + d, n)}, device_id_type=MESH
         )
 
+    pl.semaphore_signal(barrier, inc=1, device_id={"head": peer}, device_id_type=MESH)
+
     pairs = [
         (kh_h.at[:, kv_cols], kh),
         (cos_h.at[own_rows], cosine),
         (sin_h.at[own_rows], sine),
         (kgain_h, kgain),
-        (vh_h.at[:, kv_cols], vbuf.at[me]),
+        (vh_h.at[:, kv_cols], kv.at[1, me]),
         (qraw_h, qraw),
         (kraw_h, kraw),
         (vraw_h, vraw),
@@ -170,10 +189,10 @@
 
     for load in loads[:5]:
         load.wait()
-    kbuf[me] = rope_norm(kh[...].astype(F32), kgain[...], cosine[...], sine[...])
+    kv[0, me] = rope_norm(kh[...].astype(F32), kgain[...], cosine[...], sine[...])
     for load in loads[5:15]:
         load.wait()
-    pl.semaphore_wait(barrier, n - 1)
+    pl.semaphore_wait(barrier, n)
 
     def rim_copy(raw, rim, i, dest):
         return pltpu.make_async_remote_copy(
@@ -185,13 +204,23 @@
             device_id_type=MESH,
         )
 
-    def kv_copy(buf, i, block, dest):
+    def kv_copy(block, dest):
         return pltpu.make_async_remote_copy(
-            src_ref=buf.at[block],
-            dst_ref=buf.at[block],
-            send_sem=kv_send.at[i, dest],
-            recv_sem=kv_recv.at[i, block],
+            src_ref=kv.at[core, block],
+            dst_ref=kv.at[core, block],
+            send_sem=kv_send.at[dest],
+            recv_sem=kv_recv.at[block],
             device_id={"ctx": dest},
+            device_id_type=MESH,
+        )
+
+    def pass_copy(which, block):
+        return pltpu.make_async_remote_copy(
+            src_ref=kv.at[which, block],
+            dst_ref=kv.at[which, block],
+            send_sem=pass_send.at[block],
+            recv_sem=pass_recv.at[block],
+            device_id={"head": peer},
             device_id_type=MESH,
         )
 
@@ -214,17 +243,17 @@
 
     @pl.loop(me + 1, n)
     def _(dest):
-        kv_copy(kbuf, 0, me, dest).start()
-        kv_copy(vbuf, 1, me, dest).start()
+        kv_copy(me, dest).start()
 
     row, col = iotas(rows)
     ones_low = jnp.where(row >= col, 1.0, 0.0)
-    cum_s[...] = jnp.dot(ones_low, decay[...], precision=HIGHEST, preferred_element_type=F32)
     ones_up = jnp.where(row <= col, 1.0, 0.0)
-    cumt_s[...] = lax.dot_general(
-        decay[...], ones_up, (((0,), (0,)), ((), ())), precision=HIGHEST,
+    cumt_s[...] = jnp.dot(decay[...], ones_up, precision=HIGHEST, preferred_element_type=F32)
+    cum_s[...] = lax.dot_general(
+        ones_low, decay[...], (((1,), (1,)), ((), ())), precision=HIGHEST,
         preferred_element_type=F32,
     )
+    beta_s[...] = beta_in[...].T
 
     @pl.when(me == 0)
     def _():
@@ -248,23 +277,39 @@
             total = term if total is None else total + term
         return total * sigmoid(total)
 
-    def head_pair(kh_i, carry):
-        cols = pl.ds(pl.multiple_of(kh_i * D_K, D_K), D_K)
-        query = unit_rows(conv_silu(0, qraw, rim_q, cq, cols)) * D_K ** (-0.5)
-        key = unit_rows(conv_silu(1, kraw, rim_k, ck, cols))
-        key_t = key.T
-        gram = mm(key, key_t)
-        scores = mm(query, key_t)
+    group = 2 if key_heads % 2 == 0 else 1
+
+    def head_group(g, carry):
         lane = lax.broadcasted_iota(jnp.int32, (rows, value_heads), 1)
-        for r in range(REPEATS):
-            h = kh_i * REPEATS + r
-            vcols = pl.ds(pl.multiple_of(h * D_V, D_V), D_V)
-            value = conv_silu(2 + r, vraw, rim_v, cv, vcols)
-            cum = jnp.sum(jnp.where(lane == h, cum_s[...], 0.0), -1, keepdims=True)
-            beta = jnp.sum(jnp.where(lane == h, beta_in[...], 0.0), -1, keepdims=True)
-            out_local, state_query, offset, transfer = delta_local(
-                gram, scores, key, key_t, query, value, cum, cumt_s[pl.ds(h, 1), :], beta
-            )
+        mrow, mcol = iotas(rows)
+        masks = (
+            mrow >= mcol, mrow > mcol, mrow == mcol,
+            (mrow // 16) == (mcol // 16), (mrow // 64) == (mcol // 64),
+        )
+        heads = []
+        for i in range(group):
+            kh_i = g * group + i
+            cols = pl.ds(pl.multiple_of(kh_i * D_K, D_K), D_K)
+            slot = i * (2 + REPEATS)
+            query = unit_rows(conv_silu(slot, qraw, rim_q, cq, cols)) * D_K ** (-0.5)
+            key = unit_rows(conv_silu(slot + 1, kraw, rim_k, ck, cols))
+            key_t = key.T
+            gram = mm(key, key_t)
+            scores = mm(query, key_t)
+            for r in range(REPEATS):
+                h = kh_i * REPEATS + r
+                vcols = pl.ds(pl.multiple_of(h * D_V, D_V), D_V)
+                heads.append(dict(
+                    h=h, vcols=vcols, query=query, key=key, key_t=key_t, gram=gram,
+                    scores=scores,
+                    value=conv_silu(slot + 2 + r, vraw, rim_v, cv, vcols),
+                    cum=jnp.sum(jnp.where(lane == h, cum_s[...], 0.0), -1, keepdims=True),
+                    beta=jnp.sum(jnp.where(lane == h, beta_s[...], 0.0), -1, keepdims=True),
+                    cum_row=cumt_s[pl.ds(h, 1), :],
+                ))
+        results = delta_local(heads, masks)
+        for item, (out_local, state_query, offset, transfer) in zip(heads, results):
+            h, vcols = item["h"], item["vcols"]
             out_local_s[:, vcols] = out_local
             state_query_s[:, vcols] = state_query.astype(BF16)
             offset_s[h] = offset
@@ -273,12 +318,17 @@
 
         @pl.when(me == 0)
         def _():
-            for r in range(REPEATS):
-                state_copy(kh_i * REPEATS + r, later).start()
+            for i in range(group * REPEATS):
+                state_copy(g * group * REPEATS + i, later).start()
 
         return carry
 
-    lax.fori_loop(0, key_heads, head_pair, 0)
+    lax.fori_loop(0, key_heads // group, head_group, 0)
+
+    @pl.loop(0, me)
+    def _(block):
+        kv_copy(block, behind).wait_recv()
+        pass_copy(core, block).start()
 
     for load in loads[15:]:
         load.wait()
@@ -300,7 +350,7 @@
     scale = HEAD_DIM ** (-0.5)
 
     def attend(i, block, diagonal):
-        scores = mmt(qrot[i], kbuf[block]) * scale
+        scores = mmt(qrot[i], kv[0, block]) * scale
         if diagonal:
             arow, acol = iotas(rows)
             scores = jnp.where(acol <= arow, scores, -1e30)
@@ -312,7 +362,7 @@
             new = jnp.maximum(old, top)
         expos = jnp.exp(scores - new)
         total = jnp.sum(expos, -1, keepdims=True)
-        mixed = mm(expos, vbuf[block])
+        mixed = mm(expos, kv[1, block])
         if not diagonal:
             factor = jnp.exp(old - new)
             total = total + l_s[i] * factor
@@ -330,8 +380,7 @@
 
     @pl.loop(0, me)
     def _(block):
-        kv_copy(kbuf, 0, block, behind).wait_recv()
-        kv_copy(vbuf, 1, block, behind).wait_recv()
+        pass_copy(1 - core, block).wait_recv()
         for i in range(q_heads):
             attend(i, block, False)
 
@@ -370,8 +419,11 @@
 
     @pl.loop(me + 1, n)
     def _(dest):
-        kv_copy(kbuf, 0, me, dest).wait_send()
-        kv_copy(vbuf, 1, me, dest).wait_send()
+        kv_copy(me, dest).wait_send()
+
+    @pl.loop(0, me)
+    def _(block):
+        pass_copy(core, block).wait_send()
 
     at_copy.wait()
     dn_copy.wait()
@@ -400,8 +452,8 @@
     q_count = query_heads.shape[1] // HEAD_DIM
     cosine, sine = rope_tables(n * rows)
     ins = (
-        query_raw, key_raw, value_raw, out_gate, conv_query, conv_key, conv_value, decay_log,
-        write_beta, norm_gain[None], query_heads, gate_heads, key_heads, value_heads,
+        query_raw, key_raw, value_raw, out_gate, conv_query, conv_key, conv_value, decay_log.T,
+        write_beta.T, norm_gain[None], query_heads, gate_heads, key_heads, value_heads,
         query_gain[None], key_gain[None], jnp.asarray(cosine), jnp.asarray(sine),
     )
     like = lambda array: pltpu.VMEM(array.shape, array.dtype)
@@ -410,15 +462,15 @@
     scratch += [pltpu.VMEM((rows, 128), F32)] * 2
     scratch += [pltpu.VMEM((RIM, a.shape[1]), BF16) for a in ins[:3]]
     scratch += [
-        pltpu.VMEM((2 + REPEATS, RIM + rows, 128), F32),
+        pltpu.VMEM((2 * (2 + REPEATS), RIM + rows, 128), F32),
+        pltpu.VMEM((rows, value_count), F32),
         pltpu.VMEM((rows, value_count), F32),
         pltpu.VMEM((value_count, rows), F32),
         pltpu.VMEM((rows, value_count * D_V), F32),
         pltpu.VMEM((rows, value_count * D_K), BF16),
         pltpu.VMEM((value_count, D_K, D_V), F32),
         pltpu.VMEM((value_count, D_K, D_K), BF16),
-        pltpu.VMEM((n, rows, HEAD_DIM), BF16),
-        pltpu.VMEM((n, rows, HEAD_DIM), BF16),
+        pltpu.VMEM((2, n, rows, HEAD_DIM), BF16),
         pltpu.VMEM((q_count, rows, HEAD_DIM), BF16),
         pltpu.VMEM((q_count, rows, 1), F32),
         pltpu.VMEM((q_count, rows, 1), F32),
@@ -430,8 +482,10 @@
         pltpu.SemaphoreType.DMA((18,)),
         pltpu.SemaphoreType.DMA((3,)),
         pltpu.SemaphoreType.DMA((3,)),
-        pltpu.SemaphoreType.DMA((2, n)),
-        pltpu.SemaphoreType.DMA((2, n)),
+        pltpu.SemaphoreType.DMA((n,)),
+        pltpu.SemaphoreType.DMA((n,)),
+        pltpu.SemaphoreType.DMA((n,)),
+        pltpu.SemaphoreType.DMA((n,)),
         pltpu.SemaphoreType.DMA((value_count,)),
         pltpu.SemaphoreType.DMA((value_count,)),
         pltpu.SemaphoreType.DMA((2,)),
@@ -446,7 +500,7 @@
         out_specs=(pl.BlockSpec(memory_space=pl.ANY),) * 2,
         scratch_shapes=scratch,
         compiler_params=pltpu.CompilerParams(
-            collective_id=0, has_side_effects=True, vmem_limit_bytes=48 * 2**20
+            collective_id=0, has_side_effects=True, vmem_limit_bytes=60 * 2**20
         ),
         name="token_mixing",
     )(*ins)

time: 55.1 us -> 34.7 us (0.63)
  local copies, waits for them, and re-layouts: 13.8 us -> 2.72 us
  Pallas kernels: 39.9 us -> 31.2 us
    unnamed x36 -> x4, local copies, waits for them, and re-layouts: 13.8 us -> 2.72 us
    pallas_call x1, Pallas kernels: 39.9 us -> 31.2 us  [body(): pl.pallas_call(functools.partial(kernel, n), out_shape=(jax.ShapeDtypeStr...]
where the time goes in v2:
time: 34.7 us; the launch traced here: 34.6 us
  Pallas kernels  31.2 us (90%)
  local copies, waits for them, and re-layouts  2.72 us (8%)
  between operations  0.65 us (2%)
    pallas_call x1, Pallas kernels, body(): pl.pallas_call(functools.partial(kernel, n), out_shape=(jax.ShapeDtypeStr...  31.2 us
    unnamed x4, local copies, waits for them, and re-layouts  2.72 us

profile of v2, /device:TPU:24, one launch (start us, length us, event | category | flops | bytes accessed | tf_op | source)
XLA Modules:
  0.0 34.6 jit_solution(11565694264095294627)
XLA Ops:
  0.6 31.2 %token_mixing.1 = (bf16[256,1024]{1,0:T(8,128)(2,1)}, bf16[256,1024]{1,0:T(8,128)(2,1)}) custom-call(bf16[256,512]{1,0:T(8,128)(2,1)} %refs_0_.1, bf16[256,512]{1,0:T(8,128)(2,1)} %refs_1_.1, bf16[256,1024]{1,0:T(8,128)(2,1)} %refs_2_.1, bf16[256,1024]{1,0:T(8,128)(2,1)} %refs_3_.1, f32[4,512]{1,0:T(4,128)} %refs_4_.1, f32[4,512]{1,0:T(4,128)} %refs_5_.1, ...), custom_call_target="tpu_custom_call" | custom-call | tf_op jit(solution)/shard_map/token_mixing/pallas_call | solution.py:493
  31.8 0.0 copy-start
  31.8 1.9 %copy.22 = bf16[256,1024]{1,0:T(8,128)(2,1)} copy(bf16[256,1024]{1,0:T(8,128)(2,1)} %get-tuple-element.4) | data formatting | bytes 1048576
  33.8 0.0 copy-done
  33.8 0.8 %copy.23 = bf16[256,1024]{1,0:T(8,128)(2,1)} copy(bf16[256,1024]{1,0:T(8,128)(2,1)S(1)} %copy-done) | data formatting | bytes 1048576
Async XLA Ops:
  31.8 1.9 %copy-start = (bf16[256,1024]{1,0:T(8,128)(2,1)S(1)}, bf16[256,1024]{1,0:T(8,128)(2,1)}, u32[]{:S(2)}) copy-start(bf16[256,1024]{1,0:T(8,128)(2,1)} %get-tuple-element.5) | copy-start | bytes 1572868

commit v3 on v2

--- a/solution.py
+++ b/solution.py
@@ -152,11 +152,9 @@
 
     barrier = pltpu.get_barrier_semaphore()
 
-    @pl.loop(1, n)
-    def _(d):
-        pl.semaphore_signal(
-            barrier, inc=1, device_id={"ctx": lax.rem(me + d, n)}, device_id_type=MESH
-        )
+    @pl.when(me > 0)
+    def _():
+        pl.semaphore_signal(barrier, inc=1, device_id={"ctx": behind}, device_id_type=MESH)
 
     pl.semaphore_signal(barrier, inc=1, device_id={"head": peer}, device_id_type=MESH)
 
@@ -166,6 +164,8 @@
         (sin_h.at[own_rows], sine),
         (kgain_h, kgain),
         (vh_h.at[:, kv_cols], kv.at[1, me]),
+        (qgain_h, qgain),
+        (qh_h, qh),
         (qraw_h, qraw),
         (kraw_h, kraw),
         (vraw_h, vraw),
@@ -175,8 +175,6 @@
         (ck_h, ck),
         (cv_h, cv),
         (ngain_h, ngain),
-        (qgain_h, qgain),
-        (qh_h, qh),
         (gh_h, gh),
         (ogate_h, ogate),
     ]
@@ -186,13 +184,6 @@
     ]
     for load in loads:
         load.start()
-
-    for load in loads[:5]:
-        load.wait()
-    kv[0, me] = rope_norm(kh[...].astype(F32), kgain[...], cosine[...], sine[...])
-    for load in loads[5:15]:
-        load.wait()
-    pl.semaphore_wait(barrier, n)
 
     def rim_copy(raw, rim, i, dest):
         return pltpu.make_async_remote_copy(
@@ -208,7 +199,7 @@
         return pltpu.make_async_remote_copy(
             src_ref=kv.at[core, block],
             dst_ref=kv.at[core, block],
-            send_sem=kv_send.at[dest],
+            send_sem=kv_send.at[block],
             recv_sem=kv_recv.at[block],
             device_id={"ctx": dest},
             device_id_type=MESH,
@@ -234,16 +225,25 @@
             device_id_type=MESH,
         )
 
-    rims = [(qraw, rim_q), (kraw, rim_k), (vraw, rim_v)]
+    rims = [(qraw_h, rim_q), (kraw_h, rim_k), (vraw_h, rim_v)]
+
+    pl.semaphore_wait(barrier, 1 + later - me)
 
     @pl.when(me < n - 1)
     def _():
         for i, (raw, rim) in enumerate(rims):
             rim_copy(raw, rim, i, later).start()
 
-    @pl.loop(me + 1, n)
-    def _(dest):
-        kv_copy(me, dest).start()
+    for load in loads[:5]:
+        load.wait()
+    kv[0, me] = rope_norm(kh[...].astype(F32), kgain[...], cosine[...], sine[...])
+
+    @pl.when(me < n - 1)
+    def _():
+        kv_copy(me, later).start()
+
+    for load in loads[5:17]:
+        load.wait()
 
     row, col = iotas(rows)
     ones_low = jnp.where(row >= col, 1.0, 0.0)
@@ -261,8 +261,39 @@
             rim[...] = jnp.zeros_like(rim)
         in_buf[...] = jnp.zeros_like(in_buf)
 
+    scale = HEAD_DIM ** (-0.5)
+
+    def attend(i, block, diagonal):
+        scores = mmt(qrot[i], kv[0, block]) * scale
+        if diagonal:
+            arow, acol = iotas(rows)
+            scores = jnp.where(acol <= arow, scores, -1e30)
+        top = jnp.max(scores, -1, keepdims=True)
+        if diagonal:
+            new = top
+        else:
+            old = m_s[i]
+            new = jnp.maximum(old, top)
+        expos = jnp.exp(scores - new)
+        total = jnp.sum(expos, -1, keepdims=True)
+        mixed = mm(expos, kv[1, block])
+        if not diagonal:
+            factor = jnp.exp(old - new)
+            total = total + l_s[i] * factor
+            mixed = mixed + acc_s[i] * factor
+        m_s[i] = new
+        l_s[i] = total
+        acc_s[i] = mixed
+
+    def own_block():
+        for i in range(q_heads):
+            cols = slice(i * HEAD_DIM, (i + 1) * HEAD_DIM)
+            qrot[i] = rope_norm(qh[:, cols].astype(F32), qgain[...], cosine[...], sine[...])
+            attend(i, me, True)
+
     @pl.when(me > 0)
     def _():
+        own_block()
         for i, (raw, rim) in enumerate(rims):
             rim_copy(raw, rim, i, behind).wait_recv()
 
@@ -278,6 +309,16 @@
         return total * sigmoid(total)
 
     group = 2 if key_heads % 2 == 0 else 1
+    groups = key_heads // group
+
+    def ring_step(step):
+        block = me - step
+        kv_copy(block, behind).wait_recv()
+        pass_copy(core, block).start()
+
+        @pl.when(me < n - 1)
+        def _():
+            kv_copy(block, later).start()
 
     def head_group(g, carry):
         lane = lax.broadcasted_iota(jnp.int32, (rows, value_heads), 1)
@@ -321,24 +362,16 @@
             for i in range(group * REPEATS):
                 state_copy(g * group * REPEATS + i, later).start()
 
+        @pl.when(g + 1 <= me)
+        def _():
+            ring_step(g + 1)
+
         return carry
 
-    lax.fori_loop(0, key_heads // group, head_group, 0)
-
-    @pl.loop(0, me)
-    def _(block):
-        kv_copy(block, behind).wait_recv()
-        pass_copy(core, block).start()
-
-    for load in loads[15:]:
-        load.wait()
-
-    for i in range(q_heads):
-        cols = slice(i * HEAD_DIM, (i + 1) * HEAD_DIM)
-        qrot[i] = rope_norm(qh[:, cols].astype(F32), qgain[...], cosine[...], sine[...])
-
-    def relay():
-        @pl.loop(0, value_heads)
+    lax.fori_loop(0, groups, head_group, 0)
+
+    def relay(first, count):
+        @pl.loop(first, first + count)
         def _(h):
             state_copy(h, behind).wait_recv()
 
@@ -347,42 +380,36 @@
                 send_buf[h] = (mm(transfer_s[h], in_buf[h]) + offset_s[h]).astype(BF16)
                 state_copy(h, later).start()
 
-    scale = HEAD_DIM ** (-0.5)
-
-    def attend(i, block, diagonal):
-        scores = mmt(qrot[i], kv[0, block]) * scale
-        if diagonal:
-            arow, acol = iotas(rows)
-            scores = jnp.where(acol <= arow, scores, -1e30)
-        top = jnp.max(scores, -1, keepdims=True)
-        if diagonal:
-            new = top
-        else:
-            old = m_s[i]
-            new = jnp.maximum(old, top)
-        expos = jnp.exp(scores - new)
-        total = jnp.sum(expos, -1, keepdims=True)
-        mixed = mm(expos, kv[1, block])
-        if not diagonal:
-            factor = jnp.exp(old - new)
-            total = total + l_s[i] * factor
-            mixed = mixed + acc_s[i] * factor
-        m_s[i] = new
-        l_s[i] = total
-        acc_s[i] = mixed
-
-    for i in range(q_heads):
-        attend(i, me, True)
+    half = value_heads // 2
+
+    @pl.when(me == 0)
+    def _():
+        own_block()
 
     @pl.when(me == 1)
     def _():
-        relay()
-
-    @pl.loop(0, me)
-    def _(block):
-        pass_copy(1 - core, block).wait_recv()
+        relay(0, half)
+
+    @pl.loop(1, me + 1)
+    def _(step):
+        @pl.when(step > groups)
+        def _():
+            ring_step(step)
+
+        pass_copy(1 - core, me - step).wait_recv()
         for i in range(q_heads):
-            attend(i, block, False)
+            attend(i, me - step, False)
+
+    @pl.when(me > 1)
+    def _():
+        relay(0, half)
+
+    @pl.when(me > 0)
+    def _():
+        relay(half, value_heads - half)
+
+    for load in loads[17:]:
+        load.wait()
 
     for i in range(q_heads):
         cols = slice(i * HEAD_DIM, (i + 1) * HEAD_DIM)
@@ -390,10 +417,6 @@
         at_v[:, cols] = (acc_s[i] / l_s[i] * gate).astype(BF16)
     at_copy = pltpu.make_async_copy(at_v, at_out, out_sem.at[0])
     at_copy.start()
-
-    @pl.when(me > 1)
-    def _():
-        relay()
 
     gain = ngain[...]
 
@@ -417,9 +440,9 @@
         def _(h):
             state_copy(h, later).wait_send()
 
-    @pl.loop(me + 1, n)
-    def _(dest):
-        kv_copy(me, dest).wait_send()
+        @pl.loop(0, me + 1)
+        def _(block):
+            kv_copy(block, later).wait_send()
 
     @pl.loop(0, me)
     def _(block):
@@ -427,6 +450,17 @@
 
     at_copy.wait()
     dn_copy.wait()
+
+
+def place(first, second, first_out, second_out, sem):
+    copies = [
+        pltpu.make_async_copy(first, first_out, sem.at[0]),
+        pltpu.make_async_copy(second, second_out, sem.at[1]),
+    ]
+    for copy in copies:
+        copy.start()
+    for copy in copies:
+        copy.wait()
 
 
 def rope_tables(count):
@@ -490,7 +524,7 @@
         pltpu.SemaphoreType.DMA((value_count,)),
         pltpu.SemaphoreType.DMA((2,)),
     ]
-    return pl.pallas_call(
+    outs = pl.pallas_call(
         functools.partial(kernel, n),
         out_shape=(
             jax.ShapeDtypeStruct(out_gate.shape, BF16),
@@ -504,6 +538,15 @@
         ),
         name="token_mixing",
     )(*ins)
+    return pl.pallas_call(
+        place,
+        out_shape=tuple(jax.ShapeDtypeStruct(a.shape, a.dtype) for a in outs),
+        in_specs=[pl.BlockSpec(memory_space=pl.ANY)] * 2,
+        out_specs=(pl.BlockSpec(memory_space=pl.ANY),) * 2,
+        scratch_shapes=[pltpu.SemaphoreType.DMA((2,))],
+        compiler_params=pltpu.CompilerParams(vmem_limit_bytes=60 * 2**20),
+        name="place",
+    )(*outs)
 
 
 def solution(mesh):

time: 34.7 us -> 61.9 us (1.78)
  Pallas kernels: 31.2 us -> 61.1 us
  local copies, waits for them, and re-layouts: 2.72 us -> 0 us
    pallas_call x0 -> x1, Pallas kernels: none -> 32.9 us  [body(): pl.pallas_call(place, out_shape=tuple((jax.ShapeDtypeStruct(a.shape, a.dt...]
    pallas_call x1, Pallas kernels: 31.2 us -> 28.2 us  [body(): pl.pallas_call(functools.partial(kernel, n), out_shape=(jax.ShapeDtypeStr...]
    unnamed x4 -> x0, local copies, waits for them, and re-layouts: 2.72 us -> none
where the time goes in v3:
time: 61.9 us; the launch traced here: 61.7 us
  Pallas kernels  61.1 us (99%)
  between operations  0.64 us (1%)
    pallas_call x1, Pallas kernels, body(): pl.pallas_call(place, out_shape=tuple((jax.ShapeDtypeStruct(a.shape, a.dt...  32.9 us
    pallas_call x1, Pallas kernels, body(): pl.pallas_call(functools.partial(kernel, n), out_shape=(jax.ShapeDtypeStr...  28.2 us

profile of v3, /device:TPU:24, one launch (start us, length us, event | category | flops | bytes accessed | tf_op | source)
XLA Modules:
  0.0 61.7 jit_solution(923557576042821512)
XLA Ops:
  0.6 28.2 %token_mixing.1 = (bf16[256,1024]{1,0:T(8,128)(2,1)}, bf16[256,1024]{1,0:T(8,128)(2,1)}) custom-call(bf16[256,512]{1,0:T(8,128)(2,1)} %refs_0_.1, bf16[256,512]{1,0:T(8,128)(2,1)} %refs_1_.1, bf16[256,1024]{1,0:T(8,128)(2,1)} %refs_2_.1, bf16[256,1024]{1,0:T(8,128)(2,1)} %refs_3_.1, f32[4,512]{1,0:T(4,128)} %refs_4_.1, f32[4,512]{1,0:T(4,128)} %refs_5_.1, ...), custom_call_target="tpu_custom_call" | custom-call | tf_op jit(solution)/shard_map/token_mixing/pallas_call | solution.py:527
  28.8 32.9 %place.1 = (bf16[256,1024]{1,0:T(8,128)(2,1)}, bf16[256,1024]{1,0:T(8,128)(2,1)}) custom-call(bf16[256,1024]{1,0:T(8,128)(2,1)} %get-tuple-element.4.first, bf16[256,1024]{1,0:T(8,128)(2,1)} %get-tuple-element.5.second), custom_call_target="tpu_custom_call" | custom-call | tf_op jit(solution)/shard_map/place/pallas_call | solution.py:541

commit v4 on v3

--- a/solution.py
+++ b/solution.py
@@ -452,14 +452,26 @@
     dn_copy.wait()
 
 
-def place(first, second, first_out, second_out, sem):
-    copies = [
-        pltpu.make_async_copy(first, first_out, sem.at[0]),
-        pltpu.make_async_copy(second, second_out, sem.at[1]),
-    ]
-    for copy in copies:
+def place(first, second, first_out, second_out, held, sem_in, sem_out):
+    pieces = held.shape[1]
+    rows = held.shape[2]
+    arrays = [(first, first_out), (second, second_out)]
+    ins, outs = [], []
+    for i, (source, target) in enumerate(arrays):
+        for j in range(pieces):
+            part = pl.ds(j * rows, rows)
+            ins.append(
+                pltpu.make_async_copy(source.at[part], held.at[i, j], sem_in.at[i, j])
+            )
+            outs.append(
+                pltpu.make_async_copy(held.at[i, j], target.at[part], sem_out.at[i, j])
+            )
+    for copy in ins:
         copy.start()
-    for copy in copies:
+    for copy, onward in zip(ins, outs):
+        copy.wait()
+        onward.start()
+    for copy in outs:
         copy.wait()
 
 
@@ -543,7 +555,11 @@
         out_shape=tuple(jax.ShapeDtypeStruct(a.shape, a.dtype) for a in outs),
         in_specs=[pl.BlockSpec(memory_space=pl.ANY)] * 2,
         out_specs=(pl.BlockSpec(memory_space=pl.ANY),) * 2,
-        scratch_shapes=[pltpu.SemaphoreType.DMA((2,))],
+        scratch_shapes=[
+            pltpu.VMEM((2, 4, rows // 4, out_gate.shape[1]), BF16),
+            pltpu.SemaphoreType.DMA((2, 4)),
+            pltpu.SemaphoreType.DMA((2, 4)),
+        ],
         compiler_params=pltpu.CompilerParams(vmem_limit_bytes=60 * 2**20),
         name="place",
     )(*outs)

time: 61.9 us -> 31.1 us (0.50)
  Pallas kernels: 61.1 us -> 30.3 us
    pallas_call x1, Pallas kernels: 32.9 us -> 2.09 us  [body(): pl.pallas_call(place, out_shape=tuple((jax.ShapeDtypeStruct(a.shape, a.dt...]
where the time goes in v4:
time: 31.1 us; the launch traced here: 30.9 us
  Pallas kernels  30.3 us (97%)
  between operations  0.64 us (2%)
    pallas_call x1, Pallas kernels, body(): pl.pallas_call(functools.partial(kernel, n), out_shape=(jax.ShapeDtypeStr...  28.2 us
    pallas_call x1, Pallas kernels, body(): pl.pallas_call(place, out_shape=tuple((jax.ShapeDtypeStruct(a.shape, a.dt...  2.09 us

profile of v4, /device:TPU:24, one launch (start us, length us, event | category | flops | bytes accessed | tf_op | source)
XLA Modules:
  0.0 30.9 jit_solution(3132112743062019274)
XLA Ops:
  0.6 28.2 %token_mixing.1 = (bf16[256,1024]{1,0:T(8,128)(2,1)}, bf16[256,1024]{1,0:T(8,128)(2,1)}) custom-call(bf16[256,512]{1,0:T(8,128)(2,1)} %refs_0_.1, bf16[256,512]{1,0:T(8,128)(2,1)} %refs_1_.1, bf16[256,1024]{1,0:T(8,128)(2,1)} %refs_2_.1, bf16[256,1024]{1,0:T(8,128)(2,1)} %refs_3_.1, f32[4,512]{1,0:T(4,128)} %refs_4_.1, f32[4,512]{1,0:T(4,128)} %refs_5_.1, ...), custom_call_target="tpu_custom_call" | custom-call | tf_op jit(solution)/shard_map/token_mixing/pallas_call | solution.py:539
  28.8 2.1 %place.1 = (bf16[256,1024]{1,0:T(8,128)(2,1)}, bf16[256,1024]{1,0:T(8,128)(2,1)}) custom-call(bf16[256,1024]{1,0:T(8,128)(2,1)} %get-tuple-element.4.first, bf16[256,1024]{1,0:T(8,128)(2,1)} %get-tuple-element.5.second), custom_call_target="tpu_custom_call" | custom-call | tf_op jit(solution)/shard_map/place/pallas_call | solution.py:553
